TPU v7x, 512 devices: a whole 4x8x8 slice. The times are simulated.
512 devices in a mesh: section: 4 (over x), dp: 128 (over z, y, core).
Axes of the slice: x: 4, y: 8, z: 8, core: 2. Of those that a mesh axis runs over, the one named last changes fastest.
Arguments:
- saved_input: bfloat16 [4, 16384, 4096], P('section', 'dp'), may hold values from -48 to 48
- upstream: bfloat16 [4, 16384, 4096], P('section', 'dp'), may hold values from -6 to 6
- cotangent: bfloat16 [4, 16384, 4096], P('section', 'dp'), may hold values from -6 to 6
- norm_gain: bfloat16 [4, 4096], P('section'), may hold values from 0.099609375 to 1.8984375
- token_ids: int32 [16384], P('dp'), may hold values from 0 to 1023, as said below
- piece_home: int32 [1024], replicated, may hold values from 0 to 1023, as said below
- piece_table: float32 [1024, 4096], P('dp', 'section'), may hold values from -0.3 to 0.3
- first_moment: float32 [1024, 4096], P('dp', 'section'), may hold values from -2 to 2
- second_moment: float32 [1024, 4096], P('dp', 'section'), may hold values from 0.01 to 1
Outputs:
- passed_grads: bfloat16 [4, 16384, 4096], P('section', 'dp')
- fresh_rows: float32 [16384, 4096], P('dp', 'section')
- new_table: float32 [1024, 4096], P('dp', 'section')
- new_first: float32 [1024, 4096], P('dp', 'section')
- new_second: float32 [1024, 4096], P('dp', 'section')
Inputs may be any that keep to these rules, and one draw needn't show every extreme that they name: `token_ids`: among the tokens of one index of dp, at most 2 distinct pieces share a keeper piece_home // 8; on every index some keeper has exactly 2. `piece_home`: A permutation of the storage rows.
All inputs are finite; a program needn't handle non-finite values.
Results may differ from a plain program's by a relative error of at most 0.008.
Values may be sent and summed in bfloat16 or wider, within the bound.
A program may use at most 64 MiB of HBM per device.

v0:
```python
import jax
import jax.numpy as jnp
from jax import lax
from jax.sharding import PartitionSpec as P

STEP = 10


norm_eps = 1e-05
adam_eps = 1e-08
beta_one = 0.9
beta_two = 0.99
learn_rate = 0.01


def shifted(block, axis, distance):
    devices = range(lax.axis_size(axis))
    route = [(i - distance, i) for i in devices if i - distance in devices]
    return lax.ppermute(block, axis, route)


def broadcast(shard, axis, root):
    mine = lax.axis_index(axis) == root
    return lax.psum(jnp.where(mine, shard, jnp.zeros_like(shard)), axis)


def norm_backward(inputs, gain, cotangent, upstream):
    inputs = inputs.astype(jnp.float32)
    scaled = gain.astype(jnp.float32) * cotangent.astype(jnp.float32)
    inverse = lax.rsqrt(jnp.mean(inputs * inputs, axis=-1, keepdims=True) + norm_eps)
    along = jnp.mean(inputs * scaled, axis=-1, keepdims=True)
    result = upstream.astype(jnp.float32) + inverse * scaled - inputs * inverse**3 * along
    return result.astype(jnp.bfloat16)


def adam_rows(touched, grads, table, first, second):
    first_new = jnp.where(touched, beta_one * first + (1.0 - beta_one) * grads, first)
    second_new = jnp.where(touched, beta_two * second + (1.0 - beta_two) * grads * grads, second)
    fix_one = 1.0 - beta_one**STEP
    fix_two = 1.0 - beta_two**STEP
    update = learn_rate * (first_new / fix_one) / (jnp.sqrt(second_new / fix_two) + adam_eps)
    table_new = jnp.where(touched, table - update, table)
    return (table_new, first_new, second_new)


def shards(
    saved_input,
    upstream,
    cotangent,
    norm_gain,
    token_ids,
    piece_home,
    piece_table,
    first_moment,
    second_moment,
):
    input_grad = norm_backward(saved_input[0], norm_gain[0][None, :], cotangent[0], upstream[0])
    passed_grads = shifted(input_grad[None], "section", -1)
    first_grad = broadcast(input_grad, "section", 0)
    section_index = lax.axis_index("section")
    quarter = piece_table.shape[1]
    num_pieces = piece_home.shape[0]
    grad_part = lax.dynamic_slice_in_dim(first_grad, section_index * quarter, quarter, 1)
    home = jnp.take(piece_home, token_ids, axis=0)
    onehot = (home[:, None] == jnp.arange(num_pieces, dtype=jnp.int32)[None, :]).astype(
        jnp.bfloat16
    )
    piece_sums = jnp.einsum("tp,td->pd", onehot, grad_part, preferred_element_type=jnp.float32)
    piece_counts = jnp.sum(onehot.astype(jnp.float32), axis=0)
    row_grad, hits = (
        lax.psum_scatter(piece_sums, "dp", scatter_dimension=0, tiled=True),
        lax.psum_scatter(piece_counts, "dp", scatter_dimension=0, tiled=True),
    )
    touched = (hits > 0.5)[:, None]
    new_table, new_first, new_second = adam_rows(
        touched, row_grad, piece_table, first_moment, second_moment
    )
    whole_table = lax.all_gather(new_table, "dp", axis=0, tiled=True)
    fresh_rows = jnp.take(whole_table, home, axis=0)
    return (passed_grads, fresh_rows, new_table, new_first, new_second)


def solution(mesh):
    in_specs = (
        P("section", "dp", None),
        P("section", "dp", None),
        P("section", "dp", None),
        P("section", None),
        P("dp"),
        P(),
        P("dp", "section"),
        P("dp", "section"),
        P("dp", "section"),
    )
    out_specs = (
        P("section", "dp", None),
        P("dp", "section"),
        P("dp", "section"),
        P("dp", "section"),
        P("dp", "section"),
    )
    return jax.shard_map(shards, mesh=mesh, in_specs=in_specs, out_specs=out_specs, check_vma=False)
```

profile of v0, /device:TPU:1, one launch (start us, length us, event | category | flops | bytes accessed | tf_op | source)
XLA Modules:
  0.0 423.3 jit_solution(13128242640716375484)
XLA Ops:
  7.2 0.0 copy-start
  7.2 0.0 copy-start.1
  7.2 0.0 copy-start.2
  7.2 0.0 all-reduce.3.cloned.1.call-start
  7.3 0.9 mul.125
  8.1 2.1 fusion.11
  10.3 0.0 copy-done.1
  10.3 0.0 copy-done.2
  10.3 0.0 copy-start.7
  10.3 3.2 fusion.15
  13.5 0.0 all-reduce.3.cloned.1.call-update
  13.5 0.0 reduce-scatter.2.cloned.1.call-start
  13.5 0.0 copy-done.7
  13.6 0.0 copy-done
  13.6 1.0 gather_fusion
  14.6 59.7 %all-reduce.3.cloned.1.call-done = bf16[128,4096]{1,0:T(8,128)(2,1)} async-done(((bf16[128,4096]{1,0:T(8,128)(2,1)}), bf16[128,4096]{1,0:T(8,128)(2,1)}) %all-reduce.3.cloned.1.call-update) | async-done | bytes 1048592 | tf_op jit(solution)/shard_map/psum | solution.py:24
  74.3 3.7 fusion.16
  78.0 0.0 copy-start.4
  78.0 0.0 copy-start.5
  78.0 0.0 copy-start.6
  78.0 0.0 copy-start.3
  78.0 0.0 reduce-scatter.2.cloned.1.call-update
  78.0 0.0 all-gather.2.cloned.1.call-start
  78.1 1.3 dynamic-slice
  80.1 0.1 convert_reduce_fusion
  80.2 250.1 %all-reduce = f32[1024]{0:T(1024)S(1)} all-reduce(f32[1024]{0:T(1024)S(1)} %convert_reduce_fusion), channel_id=2, replica_groups=mesh['section'=4,'dp'=128] {'dp'}, use_global_device_ids=true, to_apply=%region_3.4.clone | all-reduce | flops 1024 | bytes 8192
  330.3 0.1 dynamic-slice_compare_fusion
  330.4 0.0 reduce-scatter.2.cloned.1.call-done
  330.4 0.0 copy-done.4
  330.4 0.0 copy-done.5
  330.4 0.0 copy-done.6
  330.4 1.5 subtract_select_fusion
  331.8 0.0 all-gather.2.cloned.1.call-update
  331.9 0.0 copy-done.3
  331.9 1.0 fusion.4
  332.9 1.3 collective-permute-start
  334.2 21.9 %collective-permute-done = bf16[1,128,4096]{2,1,0:T(8,128)(2,1)S(1)} collective-permute-done((bf16[1,128,4096]{2,1,0:T(8,128)(2,1)S(1)}, bf16[1,128,4096]{2,1,0:T(8,128)(2,1)S(1)}, u32[]{:S(2)}, u32[]{:S(2)}) %collective-permute-start) | collective-permute-done | bytes 1048608 | tf_op jit(solution)/shard_map/ppermute | solution.py:19
  356.1 55.6 %all-gather.2.cloned.1.call-done = f32[1024,1024]{1,0:T(8,128)} async-done(((f32[8,1024]{1,0:T(8,128)}), f32[1024,1024]{1,0:T(8,128)}) %all-gather.2.cloned.1.call-update) | async-done | bytes 4194320 | tf_op jit(solution)/shard_map/all_gather | solution.py:78
  411.7 3.2 gather_fusion.1
  414.9 0.9 broadcast_select_fusion
  415.8 1.0 copy.16
  (6 shorter events, 0.0 us)
Async XLA Ops:
  7.2 6.4 %copy-start = (s32[1024]{0:T(1024)S(1)}, s32[1024]{0:T(1024)}, u32[]{:S(2)}) copy-start(s32[1024]{0:T(1024)} %param.14) | copy-start | bytes 12292
  7.2 3.1 copy-start.1
  7.2 3.1 copy-start.2
  7.2 67.1 %all-reduce.3.cloned.1.call-start = ((), (), s32[]{:S(2)}) async-start(), calls=%async_computation.1 | async-start | bytes 2097152 | tf_op jit(solution)/shard_map/psum | solution.py:24
  10.3 3.2 copy-start.7
  13.5 316.9 %reduce-scatter.2.cloned.1.call-start = ((), (), s32[]{:S(2)}) async-start(), calls=%async_computation.2 | async-start | bytes 4227072 | tf_op jit(solution)/shard_map/reduce_scatter | solution.py:71
  78.0 252.4 %copy-start.4 = (f32[8,1024]{1,0:T(8,128)S(1)}, f32[8,1024]{1,0:T(8,128)}, u32[]{:S(2)}) copy-start(f32[8,1024]{1,0:T(8,128)} %param.15) | copy-start | bytes 98308
  78.0 252.4 %copy-start.5 = (f32[8,1024]{1,0:T(8,128)S(1)}, f32[8,1024]{1,0:T(8,128)}, u32[]{:S(2)}) copy-start(f32[8,1024]{1,0:T(8,128)} %param.16) | copy-start | bytes 98308
  78.0 252.4 %copy-start.6 = (f32[8,1024]{1,0:T(8,128)S(1)}, f32[8,1024]{1,0:T(8,128)}, u32[]{:S(2)}) copy-start(f32[8,1024]{1,0:T(8,128)} %param.17) | copy-start | bytes 98308
  78.0 253.9 %copy-start.3 = (bf16[1,128,4096]{2,1,0:T(8,128)(2,1)S(1)}, bf16[1,128,4096]{2,1,0:T(8,128)(2,1)}, u32[]{:S(2)}) copy-start(bf16[1,128,4096]{2,1,0:T(8,128)(2,1)} %param.10) | copy-start | bytes 3145732
  78.0 333.6 %all-gather.2.cloned.1.call-start = ((), (), s32[]{:S(2)}) async-start(), calls=%async_computation.3 | async-start | bytes 4227072 | tf_op jit(solution)/shard_map/all_gather | solution.py:78
  332.9 23.3 %collective-permute-start = (bf16[1,128,4096]{2,1,0:T(8,128)(2,1)S(1)}, bf16[1,128,4096]{2,1,0:T(8,128)(2,1)S(1)}, u32[]{:S(2)}, u32[]{:S(2)}) collective-permute-start(bf16[1,128,4096]{2,1,0:T(8,128)(2,1)S(1)} %fusion.4), channel_id=1, source_target_pairs={{128,0},{256,128},{384,256},{129,1},{257,129},{385,257},{130,2},{2... | collective-permute-start | bytes 3145736 | tf_op jit(solution)/shard_map/ppermute | solution.py:19
Sparse Core Ops, SparseCore 0:
  13.6 60.6 all-reduce.2
  79.3 199.2 reduce-scatter.1
  332.0 79.6 all-gather.1
where the time goes:
time: 424 us; the launch traced here: 423 us
  blocking collectives  250 us (59%)
  waiting for transfers between devices  137 us (32%)
  between operations  14.6 us (3%)
  other arithmetic  9.74 us (2%)
  local copies, waits for them, and re-layouts  6.56 us (2%)
    unnamed x1, blocking collectives  250 us
    psum x1, waiting for transfers between devices, broadcast(): return lax.psum(jnp.where(mine, shard, jnp.zeros_like(shard)), axis)  59.7 us
    all_gather x1, waiting for transfers between devices, shards(): whole_table = lax.all_gather(new_table, 'dp', axis=0, tiled=True)  55.6 us
    ppermute x1, waiting for transfers between devices, shifted(): return lax.ppermute(block, axis, route)  21.9 us
  transfers between devices with their start and end apart: 4, of which 3 were waited for; matrix products, arithmetic and copies ran while one was open for 1% of the time, Pallas kernels for 0%

commit v1 on v0

v1 whole, which is shorter than its diff:
```python
import functools
import math

import jax
import jax.numpy as jnp
from jax import lax
from jax.experimental import pallas as pl
from jax.experimental.pallas import tpu as pltpu
from jax.sharding import PartitionSpec as P

MESH = pl.DeviceIdType.MESH
STEP = 10

norm_eps = 1e-05
adam_eps = 1e-08
beta_one = 0.9
beta_two = 0.99
learn_rate = 0.01
fix_one = 1.0 - beta_one**STEP
fix_two = 1.0 - beta_two**STEP

F32 = jnp.float32
BF16 = jnp.bfloat16
ROWS = 8
LANES = 128
CHUNKS = 4


def dot(a, b):
    return jnp.dot(a, b, preferred_element_type=F32)


def one_hot(a, b):
    return jnp.where(a == b, 1.0, 0.0).astype(BF16)


def drain(ref, sem):
    pltpu.make_async_copy(ref, ref, sem).wait()


def adam_rows(touched, grads, table, first, second):
    first_new = jnp.where(touched, beta_one * first + (1.0 - beta_one) * grads, first)
    second_new = jnp.where(touched, beta_two * second + (1.0 - beta_two) * grads * grads, second)
    update = learn_rate * (first_new / fix_one) / (jnp.sqrt(second_new / fix_two) + adam_eps)
    table_new = jnp.where(touched, table - update, table)
    return (table_new, first_new, second_new)


def kernel(
    ring,
    x_hbm,
    up_hbm,
    ct_hbm,
    gain_ref,
    tok_ref,
    home_ref,
    table_ref,
    first_ref,
    second_ref,
    passed_ref,
    fresh_ref,
    new_table_ref,
    new_first_ref,
    new_second_ref,
    x_buf,
    up_buf,
    ct_buf,
    grad,
    zeros,
    grad_half,
    by_slot,
    by_token,
    meta_out,
    meta_in,
    meta_turned,
    slots_out,
    slots_in,
    part_out,
    part_in,
    rows_out,
    rows_in,
    back_out,
    back_in,
    in_sem,
    zero_sem,
    quarter_send,
    quarter_recv,
    passed_send,
    passed_recv,
    meta_send,
    meta_recv,
    slots_send,
    slots_recv,
    part_send,
    part_recv,
    rows_send,
    rows_recv,
    back_send,
    back_recv,
):
    peers = 2 * ring
    all_slots = peers * peers
    tokens, width = grad.shape
    half = grad_half.shape[2]
    quarter = 2 * half
    sections = width // quarter
    pieces = home_ref.shape[1]
    chunk = tokens // CHUNKS
    sec = lax.axis_index("section")
    dp = lax.axis_index("dp")
    z, yc = dp // peers, dp % peers
    y, core = yc // 2, yc % 2
    ring_me = (yc, z * 2 + core)
    ring_peer = (
        lambda p: z * peers + p,
        lambda p: (p // 2) * peers + y * 2 + (p % 2),
    )
    line_me = (z, y)
    line_peer = (
        lambda q: q * peers + yc,
        lambda q: z * peers + q * 2 + core,
    )

    def send(src, dst, send_sem, recv_sem, section, index):
        pltpu.make_async_remote_copy(
            src_ref=src,
            dst_ref=dst,
            send_sem=send_sem,
            recv_sem=recv_sem,
            device_id=(section, index),
            device_id_type=MESH,
        ).start()

    def to_ring(h, out, into, send_sem, recv_sem):
        mine = pl.ds(pl.multiple_of(ring_me[h] * peers, peers), peers)

        @pl.loop(1, peers)
        def _(d):
            p = (ring_me[h] + d) % peers
            theirs = pl.ds(pl.multiple_of(p * peers, peers), peers)
            send(out.at[h, theirs], into.at[h, mine], send_sem.at[h], recv_sem.at[h], sec, ring_peer[h](p))

        into[h, mine, :] = out[h, mine, :]

    def ring_wait(h, buf, sem):
        drain(buf.at[h, pl.ds(0, (peers - 1) * peers)], sem.at[h])

    loads = ((x_hbm, x_buf), (ct_hbm, ct_buf), (up_hbm, up_buf))

    def load(c, k):
        rows = pl.ds(c * chunk, chunk)
        return pltpu.make_async_copy(loads[k][0].at[0, rows], loads[k][1].at[rows], in_sem.at[c, k])

    for c in range(CHUNKS):
        for k in range(3):
            load(c, k).start()

    barrier = pltpu.get_barrier_semaphore()

    def greet(section, index):
        pl.semaphore_signal(barrier, inc=1, device_id=(section, index), device_id_type=MESH)

    @pl.loop(1, sections)
    def _(d):
        greet((sec + d) % sections, dp)

    @pl.loop(1, peers)
    def _(d):
        greet(sec, ring_peer[0]((ring_me[0] + d) % peers))

    @pl.loop(1, ring)
    def _(d):
        q = (z + d) % ring
        greet(sec, ring_peer[1](q * 2))
        greet(sec, ring_peer[1](q * 2 + 1))

    piece_of = lax.broadcasted_iota(jnp.int32, (pieces, tokens), 0)
    named = one_hot(piece_of, tok_ref[...])
    line_of = lax.broadcasted_iota(jnp.int32, (16, pieces), 0)
    home = home_ref[...]
    keeper_and_place = jnp.where(line_of == 0, home // ROWS, home % ROWS)
    found = dot(keeper_and_place.astype(F32).astype(BF16), named)
    keeper_row, place_row = found[0:1], found[1:2]
    sub = lax.broadcasted_iota(jnp.int32, (tokens, tokens), 0)
    lane = lax.broadcasted_iota(jnp.int32, (tokens, tokens), 1)

    def as_column(row):
        return jnp.sum(jnp.where(sub == lane, row, 0.0), axis=1, keepdims=True)

    keeper_col, place_col = as_column(keeper_row), as_column(place_row)
    same = keeper_col == keeper_row
    slot_row = jnp.max(jnp.where(same & (place_col < place_row), 1.0, 0.0), axis=0, keepdims=True)
    slot_col = jnp.max(jnp.where(same & (place_row < place_col), 1.0, 0.0), axis=1, keepdims=True)

    def split(keeper, h):
        keeper = keeper.astype(jnp.int32)
        kz, ky, kc = keeper // peers, (keeper // 2) % ring, keeper % 2
        return (ky, kz, kc) if h == 0 else (kz, ky, kc)

    def slot_index(keeper, slot, h):
        near, far, kc = split(keeper, h)
        return (near * 2 + kc) * peers + far * 2 + slot.astype(jnp.int32)

    slot_sub = lax.broadcasted_iota(jnp.int32, (all_slots, tokens), 0)
    slot_lane = lax.broadcasted_iota(jnp.int32, (tokens, all_slots), 1)
    place_lane = lax.broadcasted_iota(jnp.int32, (tokens, LANES), 1)
    for h in range(2):
        spread = one_hot(slot_sub, slot_index(keeper_row, slot_row, h))
        by_slot[h] = spread
        by_token[h] = one_hot(slot_lane, slot_index(keeper_col, slot_col, h))
        far_place = split(keeper_col, h)[1] * ROWS + place_col.astype(jnp.int32)
        meta_out[h] = jnp.minimum(dot(spread, one_hot(place_lane, far_place)), 1.0).astype(BF16)

    pl.semaphore_wait(barrier, (sections - 1) + (peers - 1) + 2 * (ring - 1))
    for h in range(2):
        to_ring(h, meta_out, meta_in, meta_send, meta_recv)

    @pl.when(sec == sections - 1)
    def _():
        zeros[...] = jnp.zeros_like(zeros)
        for c in range(CHUNKS):
            rows = pl.ds(c * chunk, chunk)
            pltpu.make_async_copy(zeros, passed_ref.at[0, rows], zero_sem.at[c]).start()

    step = min(512, width)
    for c in range(CHUNKS):
        for k in range(3):
            load(c, k).wait()

        @pl.loop(0, chunk // 16)
        def _(b):
            rows = pl.ds(pl.multiple_of(c * chunk + b * 16, 16), 16)
            squares = jnp.zeros((16, step), F32)
            products = jnp.zeros((16, step), F32)
            for at in range(0, width, step):
                cols = pl.ds(at, step)
                x = x_buf[rows, cols].astype(F32)
                q = gain_ref[:, cols].astype(F32) * ct_buf[rows, cols].astype(F32)
                squares += x * x
                products += x * q
            inverse = lax.rsqrt(jnp.sum(squares, axis=1, keepdims=True) / width + norm_eps)
            along = jnp.sum(products, axis=1, keepdims=True) / width
            scale = inverse * inverse * inverse * along
            for at in range(0, width, step):
                cols = pl.ds(at, step)
                x = x_buf[rows, cols].astype(F32)
                q = gain_ref[:, cols].astype(F32) * ct_buf[rows, cols].astype(F32)
                up = up_buf[rows, cols].astype(F32)
                grad[rows, cols] = (up + inverse * q - x * scale).astype(BF16)

        rows = pl.ds(c * chunk, chunk)

        @pl.when(sec == 0)
        def _():
            @pl.loop(1, sections)
            def _(d):
                cols = pl.ds(pl.multiple_of(d * quarter, LANES), half)
                send(grad.at[rows, cols], grad_half.at[0, rows], quarter_send, quarter_recv.at[0], d, dp)

            for h in range(2):
                grad_half[h, rows, :] = grad[rows, pl.ds(h * half, half)]

        @pl.when(sec > 0)
        def _():
            send(grad.at[rows], passed_ref.at[0, rows], passed_send, passed_recv, sec - 1, dp)

    @pl.when(sec == 0)
    def _():
        @pl.loop(1, sections)
        def _(d):
            cols = pl.ds(pl.multiple_of(d * quarter + half, LANES), half)
            send(grad.at[:, cols], grad_half.at[1], quarter_send, quarter_recv.at[1], d, dp)

    places = ring * ROWS
    for h in range(2):
        ring_wait(h, meta_in, meta_recv)
        turned = meta_in[h].astype(F32).T[0:places].astype(BF16)
        meta_turned[h] = turned
        if h == 0:
            part_out[h, :, pl.ds(half, LANES)] = dot(turned, jnp.ones((all_slots, LANES), BF16))

    def slots(h):
        @pl.when(sec > 0)
        def _():
            drain(grad_half.at[h], quarter_recv.at[h])

        slots_out[h] = dot(by_slot[h], grad_half[h]).astype(BF16)
        to_ring(h, slots_out, slots_in, slots_send, slots_recv)

    part_width = (half + LANES, half)

    def parts(h):
        ring_wait(h, slots_in, slots_recv)
        part_out[h, :, pl.ds(0, half)] = dot(meta_turned[h], slots_in[h])
        cols = pl.ds(0, part_width[h])

        @pl.loop(1, ring)
        def _(d):
            q = (line_me[h] + d) % ring
            theirs = pl.ds(pl.multiple_of(q * ROWS, ROWS), ROWS)
            send(
                part_out.at[h, theirs, cols],
                part_in.at[h, line_me[h], :, cols],
                part_send.at[h],
                part_recv.at[h],
                sec,
                line_peer[h](q),
            )

        mine = pl.ds(pl.multiple_of(line_me[h] * ROWS, ROWS), ROWS)
        part_in[h, line_me[h], :, cols] = part_out[h, mine, cols]

    def update(h, hits):
        drain(part_in.at[h, pl.ds(0, ring - 1), :, pl.ds(0, part_width[h])], part_recv.at[h])
        total = part_in[h, 0]
        for q in range(1, ring):
            total += part_in[h, q]
        if h == 0:
            hits = total[:, half : half + 1]
        cols = pl.ds(h * half, half)
        table, first, second = adam_rows(
            hits > 0.5, total[:, 0:half], table_ref[:, cols], first_ref[:, cols], second_ref[:, cols]
        )
        new_table_ref[:, cols] = table
        new_first_ref[:, cols] = first
        new_second_ref[:, cols] = second
        mid = half // 2
        rows_out[h] = jnp.concatenate([table[:, 0:mid], table[:, mid:half]], axis=0).astype(BF16)

        @pl.loop(1, ring)
        def _(d):
            q = (line_me[h] + d) % ring
            send(
                rows_out.at[h],
                rows_in.at[h, line_me[h]],
                rows_send.at[h],
                rows_recv.at[h],
                sec,
                line_peer[h](q),
            )

        rows_in[h, line_me[h]] = rows_out[h]
        return hits

    def give_back(h):
        drain(rows_in.at[h, pl.ds(0, ring - 1)], rows_recv.at[h])
        blocks = []
        for q in range(ring):
            packed = rows_in[h, q].astype(F32)
            blocks.append(jnp.concatenate([packed[0:ROWS], packed[ROWS : 2 * ROWS]], axis=1))
        table = jnp.concatenate(blocks, axis=0).astype(BF16)
        back_out[h] = dot(meta_in[h, :, pl.ds(0, places)], table).astype(BF16)
        to_ring(h, back_out, back_in, back_send, back_recv)

    def fresh(h):
        ring_wait(h, back_in, back_recv)
        fresh_ref[:, pl.ds(h * half, half)] = dot(by_token[h], back_in[h])

    slots(0)
    slots(1)
    parts(0)
    hits = update(0, None)
    parts(1)
    give_back(0)
    update(1, hits)
    give_back(1)
    fresh(0)
    fresh(1)

    @pl.when(sec == 0)
    def _():
        drain(grad.at[:, pl.ds(0, width - quarter)], quarter_send)

    @pl.when(sec > 0)
    def _():
        drain(grad, passed_send)

    @pl.when(sec < sections - 1)
    def _():
        drain(passed_ref.at[0], passed_recv)

    @pl.when(sec == sections - 1)
    def _():
        for c in range(CHUNKS):
            rows = pl.ds(c * chunk, chunk)
            pltpu.make_async_copy(zeros, passed_ref.at[0, rows], zero_sem.at[c]).wait()

    for h in range(2):
        ring_wait(h, meta_out, meta_send)
        ring_wait(h, slots_out, slots_send)
        ring_wait(h, back_out, back_send)
        drain(part_in.at[h, pl.ds(0, ring - 1), :, pl.ds(0, part_width[h])], part_send.at[h])
        drain(rows_in.at[h, pl.ds(0, ring - 1)], rows_send.at[h])


def shards(
    ring,
    saved_input,
    upstream,
    cotangent,
    norm_gain,
    token_ids,
    piece_home,
    piece_table,
    first_moment,
    second_moment,
):
    _, tokens, width = saved_input.shape
    rows, quarter = piece_table.shape
    half = quarter // 2
    peers = 2 * ring
    slots = peers * peers
    anywhere = pl.BlockSpec(memory_space=pl.ANY)
    vmem = pl.BlockSpec(memory_space=pltpu.VMEM)
    dma = pltpu.SemaphoreType.DMA
    small = jax.ShapeDtypeStruct((rows, quarter), F32)
    return pl.pallas_call(
        functools.partial(kernel, ring),
        out_shape=(
            jax.ShapeDtypeStruct((1, tokens, width), BF16),
            jax.ShapeDtypeStruct((tokens, quarter), F32),
            small,
            small,
            small,
        ),
        in_specs=[anywhere] * 3 + [vmem] * 6,
        out_specs=(anywhere, vmem, vmem, vmem, vmem),
        scratch_shapes=[
            pltpu.VMEM((tokens, width), BF16),
            pltpu.VMEM((tokens, width), BF16),
            pltpu.VMEM((tokens, width), BF16),
            pltpu.VMEM((tokens, width), BF16),
            pltpu.VMEM((tokens // CHUNKS, width), BF16),
            pltpu.VMEM((2, tokens, half), BF16),
            pltpu.VMEM((2, slots, tokens), BF16),
            pltpu.VMEM((2, tokens, slots), BF16),
            pltpu.VMEM((2, slots, LANES), BF16),
            pltpu.VMEM((2, slots, LANES), BF16),
            pltpu.VMEM((2, ring * ROWS, slots), BF16),
            pltpu.VMEM((2, slots, half), BF16),
            pltpu.VMEM((2, slots, half), BF16),
            pltpu.VMEM((2, ring * ROWS, half + LANES), F32),
            pltpu.VMEM((2, ring, ROWS, half + LANES), F32),
            pltpu.VMEM((2, 2 * ROWS, half // 2), BF16),
            pltpu.VMEM((2, ring, 2 * ROWS, half // 2), BF16),
            pltpu.VMEM((2, slots, half), BF16),
            pltpu.VMEM((2, slots, half), BF16),
            dma((CHUNKS, 3)),
            dma((CHUNKS,)),
            dma,
            dma((2,)),
            dma,
            dma,
        ]
        + [dma((2,))] * 10,
        compiler_params=pltpu.CompilerParams(
            collective_id=0, has_side_effects=True, vmem_limit_bytes=40 * 2**20
        ),
        cost_estimate=pl.CostEstimate(
            flops=2 * 10**8, bytes_accessed=6 * 2**20, transcendentals=0
        ),
    )(
        saved_input,
        upstream,
        cotangent,
        norm_gain,
        token_ids[None, :],
        piece_home[None, :],
        piece_table,
        first_moment,
        second_moment,
    )


def solution(mesh):
    ring = math.isqrt(mesh.shape["dp"] // 2)
    in_specs = (
        P("section", "dp", None),
        P("section", "dp", None),
        P("section", "dp", None),
        P("section", None),
        P("dp"),
        P(),
        P("dp", "section"),
        P("dp", "section"),
        P("dp", "section"),
    )
    out_specs = (
        P("section", "dp", None),
        P("dp", "section"),
        P("dp", "section"),
        P("dp", "section"),
        P("dp", "section"),
    )
    return jax.shard_map(
        functools.partial(shards, ring),
        mesh=mesh,
        in_specs=in_specs,
        out_specs=out_specs,
        check_vma=False,
    )
```

time: 424 us -> 73.9 us (0.17)
  the two profiles are of different devices: /device:TPU:1 before, /device:TPU:5 now
where the time goes in v1:
time: 73.9 us; the launch traced here: 73.4 us
  Pallas kernels  61.1 us (83%)
  local copies, waits for them, and re-layouts  11.6 us (16%)
    pallas_call x1, Pallas kernels, shards(): pl.pallas_call(functools.partial(kernel, ring), out_shape=(jax.ShapeDtype...  61.1 us
    unnamed x23, local copies, waits for them, and re-layouts  11.6 us

profile of v1, /device:TPU:5, one launch (start us, length us, event | category | flops | bytes accessed | tf_op | source)
XLA Modules:
  0.0 73.4 jit_solution(2459290055441669934)
XLA Ops:
  0.6 0.0 copy-start.8
  0.6 0.6 copy-done.8
  1.3 0.0 copy-start
  1.3 1.2 %copy-done = bf16[1,128,4096]{2,1,0:T(8,128)(2,1)S(1)} copy-done((bf16[1,128,4096]{2,1,0:T(8,128)(2,1)S(1)}, bf16[1,128,4096]{2,1,0:T(8,128)(2,1)}, u32[]{:S(2)}) %copy-start) | copy-done | bytes 1048600
  2.5 0.0 copy-start.1
  2.5 1.2 %copy-done.1 = bf16[1,128,4096]{2,1,0:T(8,128)(2,1)S(1)} copy-done((bf16[1,128,4096]{2,1,0:T(8,128)(2,1)S(1)}, bf16[1,128,4096]{2,1,0:T(8,128)(2,1)}, u32[]{:S(2)}) %copy-start.1) | copy-done | bytes 1048600
  3.7 0.0 copy-start.2
  3.7 1.2 %copy-done.2 = bf16[1,128,4096]{2,1,0:T(8,128)(2,1)S(1)} copy-done((bf16[1,128,4096]{2,1,0:T(8,128)(2,1)S(1)}, bf16[1,128,4096]{2,1,0:T(8,128)(2,1)}, u32[]{:S(2)}) %copy-start.2) | copy-done | bytes 1048600
  5.0 0.0 copy-start.3
  5.0 0.8 %copy-done.3 = f32[8,1024]{1,0:T(8,128)S(1)} copy-done((f32[8,1024]{1,0:T(8,128)S(1)}, f32[8,1024]{1,0:T(8,128)}, u32[]{:S(2)}) %copy-start.3) | copy-done | bytes 32792
  5.7 0.0 copy-start.4
  5.7 0.8 %copy-done.4 = f32[8,1024]{1,0:T(8,128)S(1)} copy-done((f32[8,1024]{1,0:T(8,128)S(1)}, f32[8,1024]{1,0:T(8,128)}, u32[]{:S(2)}) %copy-start.4) | copy-done | bytes 32792
  6.5 0.0 copy-start.5
  6.5 0.8 %copy-done.5 = f32[8,1024]{1,0:T(8,128)S(1)} copy-done((f32[8,1024]{1,0:T(8,128)S(1)}, f32[8,1024]{1,0:T(8,128)}, u32[]{:S(2)}) %copy-start.5) | copy-done | bytes 32792
  7.2 0.0 copy-start.6
  7.2 0.7 copy-done.6
  8.0 0.0 copy-start.7
  8.0 0.7 copy-done.7
  8.6 61.1 %shard_map.128 = (bf16[1,128,4096]{2,1,0:T(8,128)(2,1)S(1)}, f32[128,1024]{1,0:T(8,128)S(1)}, f32[8,1024]{1,0:T(8,128)S(1)}, f32[8,1024]{1,0:T(8,128)S(1)}, f32[8,1024]{1,0:T(8,128)S(1)}) custom-call(bf16[1,128,4096]{2,1,0:T(8,128)(2,1)S(1)} %copy-done, bf16[1,128,4096]{2,1,0:T(8,128)(2,1)S(1)} %copy-done.1, bf16[1,128,4096]{2,1,0:T(8,128)(2,1)S(1)} %copy-done.2, ...), custom_call_target="tpu_custom_call" | custom-call | flops 200000000 | bytes 6291456 | tf_op jit(solution)/shard_map/pallas_call | solution.py:417
  69.8 1.0 %copy.19 = bf16[1,128,4096]{2,1,0:T(8,128)(2,1)} copy(bf16[1,128,4096]{2,1,0:T(8,128)(2,1)S(1)} %get-tuple-element.10) | data formatting | bytes 2097152
  70.8 0.8 %copy.20 = f32[128,1024]{1,0:T(8,128)} copy(f32[128,1024]{1,0:T(8,128)S(1)} %get-tuple-element.11) | data formatting | bytes 1048576
  71.5 0.6 copy.21
  72.2 0.6 copy.22
  72.8 0.6 copy.23
Async XLA Ops:
  0.6 0.7 copy-start.8
  1.3 1.2 %copy-start = (bf16[1,128,4096]{2,1,0:T(8,128)(2,1)S(1)}, bf16[1,128,4096]{2,1,0:T(8,128)(2,1)}, u32[]{:S(2)}) copy-start(bf16[1,128,4096]{2,1,0:T(8,128)(2,1)} %x_hbm.1) | copy-start | bytes 3145732
  2.5 1.2 %copy-start.1 = (bf16[1,128,4096]{2,1,0:T(8,128)(2,1)S(1)}, bf16[1,128,4096]{2,1,0:T(8,128)(2,1)}, u32[]{:S(2)}) copy-start(bf16[1,128,4096]{2,1,0:T(8,128)(2,1)} %up_hbm.1) | copy-start | bytes 3145732
  3.7 1.2 %copy-start.2 = (bf16[1,128,4096]{2,1,0:T(8,128)(2,1)S(1)}, bf16[1,128,4096]{2,1,0:T(8,128)(2,1)}, u32[]{:S(2)}) copy-start(bf16[1,128,4096]{2,1,0:T(8,128)(2,1)} %ct_hbm.1) | copy-start | bytes 3145732
  5.0 0.8 %copy-start.3 = (f32[8,1024]{1,0:T(8,128)S(1)}, f32[8,1024]{1,0:T(8,128)}, u32[]{:S(2)}) copy-start(f32[8,1024]{1,0:T(8,128)} %table_ref.1) | copy-start | bytes 98308
  5.7 0.8 %copy-start.4 = (f32[8,1024]{1,0:T(8,128)S(1)}, f32[8,1024]{1,0:T(8,128)}, u32[]{:S(2)}) copy-start(f32[8,1024]{1,0:T(8,128)} %first_ref.1) | copy-start | bytes 98308
  6.5 0.8 %copy-start.5 = (f32[8,1024]{1,0:T(8,128)S(1)}, f32[8,1024]{1,0:T(8,128)}, u32[]{:S(2)}) copy-start(f32[8,1024]{1,0:T(8,128)} %second_ref.1) | copy-start | bytes 98308
  7.2 0.7 copy-start.6
  8.0 0.7 copy-start.7

commit v2 on v1

--- a/solution.py
+++ b/solution.py
@@ -51,12 +51,12 @@
     x_hbm,
     up_hbm,
     ct_hbm,
-    gain_ref,
-    tok_ref,
-    home_ref,
-    table_ref,
-    first_ref,
-    second_ref,
+    gain_hbm,
+    tok_hbm,
+    home_hbm,
+    table_hbm,
+    first_hbm,
+    second_hbm,
     passed_ref,
     fresh_ref,
     new_table_ref,
@@ -65,6 +65,12 @@
     x_buf,
     up_buf,
     ct_buf,
+    gain_ref,
+    tok_ref,
+    home_ref,
+    table_ref,
+    first_ref,
+    second_ref,
     grad,
     zeros,
     grad_half,
@@ -82,6 +88,7 @@
     back_out,
     back_in,
     in_sem,
+    small_sem,
     zero_sem,
     quarter_send,
     quarter_recv,
@@ -151,9 +158,28 @@
         rows = pl.ds(c * chunk, chunk)
         return pltpu.make_async_copy(loads[k][0].at[0, rows], loads[k][1].at[rows], in_sem.at[c, k])
 
+    small = [
+        pltpu.make_async_copy(src, dst, small_sem.at[k])
+        for k, (src, dst) in enumerate(
+            (
+                (tok_hbm, tok_ref),
+                (home_hbm, home_ref),
+                (gain_hbm, gain_ref),
+                (table_hbm, table_ref),
+                (first_hbm, first_ref),
+                (second_hbm, second_ref),
+            )
+        )
+    ]
+    for copy in small[:2]:
+        copy.start()
     for c in range(CHUNKS):
         for k in range(3):
             load(c, k).start()
+        if c == 0:
+            small[2].start()
+    for copy in small[3:]:
+        copy.start()
 
     barrier = pltpu.get_barrier_semaphore()
 
@@ -173,6 +199,9 @@
         q = (z + d) % ring
         greet(sec, ring_peer[1](q * 2))
         greet(sec, ring_peer[1](q * 2 + 1))
+
+    small[0].wait()
+    small[1].wait()
 
     piece_of = lax.broadcasted_iota(jnp.int32, (pieces, tokens), 0)
     named = one_hot(piece_of, tok_ref[...])
@@ -223,6 +252,7 @@
             pltpu.make_async_copy(zeros, passed_ref.at[0, rows], zero_sem.at[c]).start()
 
     step = min(512, width)
+    small[2].wait()
     for c in range(CHUNKS):
         for k in range(3):
             load(c, k).wait()
@@ -358,6 +388,8 @@
 
     slots(0)
     slots(1)
+    for copy in small[3:]:
+        copy.wait()
     parts(0)
     hits = update(0, None)
     parts(1)
@@ -391,6 +423,15 @@
         ring_wait(h, back_out, back_send)
         drain(part_in.at[h, pl.ds(0, ring - 1), :, pl.ds(0, part_width[h])], part_send.at[h])
         drain(rows_in.at[h, pl.ds(0, ring - 1)], rows_send.at[h])
+
+
+def hand_out(*refs):
+    ins, outs, sems = refs[:5], refs[5:10], refs[10]
+    copies = [pltpu.make_async_copy(a, b, sems.at[k]) for k, (a, b) in enumerate(zip(ins, outs))]
+    for copy in copies:
+        copy.start()
+    for copy in copies:
+        copy.wait()
 
 
 def shards(
@@ -410,25 +451,44 @@
     half = quarter // 2
     peers = 2 * ring
     slots = peers * peers
+    hbm = pl.BlockSpec(memory_space=pltpu.HBM)
     anywhere = pl.BlockSpec(memory_space=pl.ANY)
     vmem = pl.BlockSpec(memory_space=pltpu.VMEM)
     dma = pltpu.SemaphoreType.DMA
     small = jax.ShapeDtypeStruct((rows, quarter), F32)
-    return pl.pallas_call(
+    out_shape = (
+        jax.ShapeDtypeStruct((1, tokens, width), BF16),
+        jax.ShapeDtypeStruct((tokens, quarter), F32),
+        small,
+        small,
+        small,
+    )
+    arrays = (
+        saved_input,
+        upstream,
+        cotangent,
+        norm_gain,
+        token_ids[None, :],
+        piece_home[None, :],
+        piece_table,
+        first_moment,
+        second_moment,
+    )
+    results = pl.pallas_call(
         functools.partial(kernel, ring),
-        out_shape=(
-            jax.ShapeDtypeStruct((1, tokens, width), BF16),
-            jax.ShapeDtypeStruct((tokens, quarter), F32),
-            small,
-            small,
-            small,
-        ),
-        in_specs=[anywhere] * 3 + [vmem] * 6,
+        out_shape=out_shape,
+        in_specs=[hbm] * 9,
         out_specs=(anywhere, vmem, vmem, vmem, vmem),
         scratch_shapes=[
             pltpu.VMEM((tokens, width), BF16),
             pltpu.VMEM((tokens, width), BF16),
             pltpu.VMEM((tokens, width), BF16),
+            pltpu.VMEM((1, width), BF16),
+            pltpu.VMEM((1, tokens), jnp.int32),
+            pltpu.VMEM((1, piece_home.shape[0]), jnp.int32),
+            pltpu.VMEM((rows, quarter), F32),
+            pltpu.VMEM((rows, quarter), F32),
+            pltpu.VMEM((rows, quarter), F32),
             pltpu.VMEM((tokens, width), BF16),
             pltpu.VMEM((tokens // CHUNKS, width), BF16),
             pltpu.VMEM((2, tokens, half), BF16),
@@ -446,6 +506,7 @@
             pltpu.VMEM((2, slots, half), BF16),
             pltpu.VMEM((2, slots, half), BF16),
             dma((CHUNKS, 3)),
+            dma((6,)),
             dma((CHUNKS,)),
             dma,
             dma((2,)),
@@ -459,17 +520,16 @@
         cost_estimate=pl.CostEstimate(
             flops=2 * 10**8, bytes_accessed=6 * 2**20, transcendentals=0
         ),
-    )(
-        saved_input,
-        upstream,
-        cotangent,
-        norm_gain,
-        token_ids[None, :],
-        piece_home[None, :],
-        piece_table,
-        first_moment,
-        second_moment,
-    )
+    )(*(pltpu.with_memory_space_constraint(array, pltpu.HBM) for array in arrays))
+    return pl.pallas_call(
+        hand_out,
+        out_shape=out_shape,
+        in_specs=[anywhere] * 5,
+        out_specs=(hbm,) * 5,
+        scratch_shapes=[dma((5,))],
+        compiler_params=pltpu.CompilerParams(vmem_limit_bytes=40 * 2**20),
+        cost_estimate=pl.CostEstimate(flops=0, bytes_accessed=3 * 2**20, transcendentals=0),
+    )(*results)
 
 
 def solution(mesh):

time: 73.9 us -> 62.5 us (0.85)
  local copies, waits for them, and re-layouts: 11.6 us -> 0 us
    unnamed x23 -> x0, local copies, waits for them, and re-layouts: 11.6 us -> none
    pallas_call x1 -> x2, Pallas kernels: 61.1 us -> 61.7 us  [the longest x1 60.5 us: shards(): pl.pallas_call(functools.partial(kernel, ring), out_shape=out_shape, in_s...]
where the time goes in v2:
time: 62.5 us; the launch traced here: 62.4 us
  Pallas kernels  61.7 us (99%)
  between operations  0.64 us (1%)
    pallas_call x1, Pallas kernels, shards(): pl.pallas_call(functools.partial(kernel, ring), out_shape=out_shape, in_s...  60.5 us

profile of v2, /device:TPU:5, one launch (start us, length us, event | category | flops | bytes accessed | tf_op | source)
XLA Modules:
  0.0 62.4 jit_solution(10117211939645912261)
XLA Ops:
  0.6 60.5 %shard_map.128 = (bf16[1,128,4096]{2,1,0:T(8,128)(2,1)S(1)}, f32[128,1024]{1,0:T(8,128)S(1)}, f32[8,1024]{1,0:T(8,128)S(1)}, f32[8,1024]{1,0:T(8,128)S(1)}, f32[8,1024]{1,0:T(8,128)S(1)}) custom-call(bf16[1,128,4096]{2,1,0:T(8,128)(2,1)} %x_hbm.1, bf16[1,128,4096]{2,1,0:T(8,128)(2,1)} %up_hbm.1, bf16[1,128,4096]{2,1,0:T(8,128)(2,1)} %ct_hbm.1, ...), custom_call_target="tpu_custom_call" | custom-call | flops 200000000 | bytes 6291456 | tf_op jit(solution)/shard_map/pallas_call | solution.py:477
  61.2 1.2 %shard_map.129 = (bf16[1,128,4096]{2,1,0:T(8,128)(2,1)}, f32[128,1024]{1,0:T(8,128)}, f32[8,1024]{1,0:T(8,128)}, f32[8,1024]{1,0:T(8,128)}, f32[8,1024]{1,0:T(8,128)}) custom-call(bf16[1,128,4096]{2,1,0:T(8,128)(2,1)S(1)} %get-tuple-element.10.refs_0_, f32[128,1024]{1,0:T(8,128)S(1)} %get-tuple-element.11.refs_1_, f32[8,1024]{1,0:T(8,128)S(1)} %get-tuple-element.12.refs_2_, ...), custom_call_target="tpu_custom_call" | custom-call | bytes 3145728 | tf_op jit(solution)/shard_map/pallas_call | solution.py:524

commit v3 on v2

v3 whole, which is shorter than its diff:
```python
import functools
import math

import jax
import jax.numpy as jnp
from jax import lax
from jax.experimental import pallas as pl
from jax.experimental.pallas import tpu as pltpu
from jax.sharding import PartitionSpec as P

MESH = pl.DeviceIdType.MESH
STEP = 10

norm_eps = 1e-05
adam_eps = 1e-08
beta_one = 0.9
beta_two = 0.99
learn_rate = 0.01
fix_one = 1.0 - beta_one**STEP
fix_two = 1.0 - beta_two**STEP

F32 = jnp.float32
BF16 = jnp.bfloat16
ROWS = 8
LANES = 128
CHUNKS = 4
PARTS = 4


def dot(a, b):
    return jnp.dot(a, b, preferred_element_type=F32)


def one_hot(a, b):
    return jnp.where(a == b, 1.0, 0.0).astype(BF16)


def drain(ref, sem):
    pltpu.make_async_copy(ref, ref, sem).wait()


def adam_rows(touched, grads, table, first, second):
    first_new = jnp.where(touched, beta_one * first + (1.0 - beta_one) * grads, first)
    second_new = jnp.where(touched, beta_two * second + (1.0 - beta_two) * grads * grads, second)
    update = learn_rate * (first_new / fix_one) / (jnp.sqrt(second_new / fix_two) + adam_eps)
    table_new = jnp.where(touched, table - update, table)
    return (table_new, first_new, second_new)


def kernel(
    ring,
    x_hbm,
    up_hbm,
    ct_hbm,
    gain_hbm,
    tok_hbm,
    home_hbm,
    table_hbm,
    first_hbm,
    second_hbm,
    passed_ref,
    fresh_ref,
    new_table_ref,
    new_first_ref,
    new_second_ref,
    x_buf,
    up_buf,
    ct_buf,
    gain_ref,
    tok_ref,
    home_ref,
    table_ref,
    first_ref,
    second_ref,
    grad,
    zeros,
    grad_part,
    by_slot,
    by_token,
    meta_out,
    meta_in,
    meta_turned,
    slots_out,
    slots_in,
    part_out,
    part_in,
    rows_out,
    rows_in,
    back_out,
    back_in,
    in_sem,
    small_sem,
    zero_sem,
    quarter_send,
    quarter_recv,
    passed_send,
    passed_recv,
    meta_send,
    meta_recv,
    slots_send,
    slots_recv,
    part_send,
    part_recv,
    rows_send,
    rows_recv,
    back_send,
    back_recv,
):
    peers = 2 * ring
    all_slots = peers * peers
    places = ring * ROWS
    tokens, width = grad.shape
    part = grad_part.shape[2]
    mid = part // 2
    quarter = PARTS * part
    sections = width // quarter
    pieces = home_ref.shape[1]
    chunk = tokens // CHUNKS
    sec = lax.axis_index("section")
    dp = lax.axis_index("dp")
    z, yc = dp // peers, dp % peers
    y, core = yc // 2, yc % 2
    ring_me = (yc, z * 2 + core)
    ring_peer = (
        lambda p: z * peers + p,
        lambda p: (p // 2) * peers + y * 2 + (p % 2),
    )
    line_me = (z, y)
    line_peer = (
        lambda q: q * peers + yc,
        lambda q: z * peers + q * 2 + core,
    )

    def send(src, dst, send_sem, recv_sem, section, index):
        pltpu.make_async_remote_copy(
            src_ref=src,
            dst_ref=dst,
            send_sem=send_sem,
            recv_sem=recv_sem,
            device_id=(section, index),
            device_id_type=MESH,
        ).start()

    def farthest_first(k, n):
        return n // 2 + (1 - 2 * (k % 2)) * ((k + 1) // 2)

    def to_ring(way, j, out, into, send_sem, recv_sem):
        mine = pl.ds(pl.multiple_of(ring_me[way] * peers, peers), peers)

        @pl.loop(0, peers - 1)
        def _(k):
            p = (ring_me[way] + farthest_first(k, peers)) % peers
            theirs = pl.ds(pl.multiple_of(p * peers, peers), peers)
            send(out.at[j, theirs], into.at[j, mine], send_sem.at[j], recv_sem.at[j], sec, ring_peer[way](p))

        into[j, mine, :] = out[j, mine, :]

    def ring_wait(j, buf, sem):
        drain(buf.at[j, pl.ds(0, (peers - 1) * peers)], sem.at[j])

    barrier = pltpu.get_barrier_semaphore()

    def greet(section, index):
        pl.semaphore_signal(barrier, inc=1, device_id=(section, index), device_id_type=MESH)

    @pl.loop(1, sections)
    def _(d):
        greet((sec + d) % sections, dp)

    @pl.loop(1, peers)
    def _(d):
        greet(sec, ring_peer[0]((ring_me[0] + d) % peers))

    @pl.loop(1, ring)
    def _(d):
        q = (z + d) % ring
        greet(sec, ring_peer[1](q * 2))
        greet(sec, ring_peer[1](q * 2 + 1))

    loads = ((x_hbm, x_buf), (ct_hbm, ct_buf), (up_hbm, up_buf))

    def load(c, k):
        rows = pl.ds(c * chunk, chunk)
        return pltpu.make_async_copy(loads[k][0].at[0, rows], loads[k][1].at[rows], in_sem.at[c, k])

    small = [
        pltpu.make_async_copy(src, dst, small_sem.at[k])
        for k, (src, dst) in enumerate(
            (
                (gain_hbm, gain_ref),
                (tok_hbm, tok_ref),
                (home_hbm, home_ref),
                (table_hbm, table_ref),
                (first_hbm, first_ref),
                (second_hbm, second_ref),
            )
        )
    ]
    small[0].start()
    for c in range(CHUNKS):
        for k in range(3):
            load(c, k).start()
    for copy in small[1:]:
        copy.start()

    step = min(512, width)

    def norm(c):
        for k in range(3):
            load(c, k).wait()

        @pl.loop(0, chunk // 16)
        def _(b):
            rows = pl.ds(pl.multiple_of(c * chunk + b * 16, 16), 16)
            squares = jnp.zeros((16, step), F32)
            products = jnp.zeros((16, step), F32)
            for at in range(0, width, step):
                cols = pl.ds(at, step)
                x = x_buf[rows, cols].astype(F32)
                q = gain_ref[:, cols].astype(F32) * ct_buf[rows, cols].astype(F32)
                squares += x * x
                products += x * q
            inverse = lax.rsqrt(jnp.sum(squares, axis=1, keepdims=True) / width + norm_eps)
            along = jnp.sum(products, axis=1, keepdims=True) / width
            scale = inverse * inverse * inverse * along
            for at in range(0, width, step):
                cols = pl.ds(at, step)
                x = x_buf[rows, cols].astype(F32)
                q = gain_ref[:, cols].astype(F32) * ct_buf[rows, cols].astype(F32)
                up = up_buf[rows, cols].astype(F32)
                grad[rows, cols] = (up + inverse * q - x * scale).astype(BF16)

    small[0].wait()
    for c in range(CHUNKS):
        norm(c)
    pl.semaphore_wait(barrier, (sections - 1) + (peers - 1) + 2 * (ring - 1))

    last = sections - 1

    def send_quarter(d, j):
        cols = pl.ds(d * quarter + j * part, part)
        send(grad.at[:, cols], grad_part.at[j], quarter_send, quarter_recv.at[j], d, dp)

    @pl.when(sec == 0)
    def _():
        for j in range(PARTS):
            for d in range(1, sections):
                send_quarter(d, j)
        for j in range(PARTS):
            grad_part[j] = grad[:, pl.ds(j * part, part)]

    @pl.when(sec > 0)
    def _():
        send(grad, passed_ref.at[0], passed_send, passed_recv, sec - 1, dp)

    small[1].wait()
    small[2].wait()
    piece_of = lax.broadcasted_iota(jnp.int32, (pieces, tokens), 0)
    named = one_hot(piece_of, tok_ref[...])
    line_of = lax.broadcasted_iota(jnp.int32, (16, pieces), 0)
    home = home_ref[...]
    keeper_and_place = jnp.where(line_of == 0, home // ROWS, home % ROWS)
    found = dot(keeper_and_place.astype(F32).astype(BF16), named)
    keeper_row, place_row = found[0:1], found[1:2]
    sub = lax.broadcasted_iota(jnp.int32, (tokens, tokens), 0)
    lane = lax.broadcasted_iota(jnp.int32, (tokens, tokens), 1)

    def as_column(row):
        return jnp.sum(jnp.where(sub == lane, row, 0.0), axis=1, keepdims=True)

    keeper_col, place_col = as_column(keeper_row), as_column(place_row)
    same = keeper_col == keeper_row
    slot_row = jnp.max(jnp.where(same & (place_col < place_row), 1.0, 0.0), axis=0, keepdims=True)
    slot_col = jnp.max(jnp.where(same & (place_row < place_col), 1.0, 0.0), axis=1, keepdims=True)

    def split(keeper, way):
        keeper = keeper.astype(jnp.int32)
        kz, ky, kc = keeper // peers, (keeper // 2) % ring, keeper % 2
        return (ky, kz, kc) if way == 0 else (kz, ky, kc)

    def slot_index(keeper, slot, way):
        near, far, kc = split(keeper, way)
        return (near * 2 + kc) * peers + far * 2 + slot.astype(jnp.int32)

    slot_sub = lax.broadcasted_iota(jnp.int32, (all_slots, tokens), 0)
    slot_lane = lax.broadcasted_iota(jnp.int32, (tokens, all_slots), 1)
    place_lane = lax.broadcasted_iota(jnp.int32, (tokens, LANES), 1)
    for way in range(2):
        spread = one_hot(slot_sub, slot_index(keeper_row, slot_row, way))
        by_slot[way] = spread
        far_place = split(keeper_col, way)[1] * ROWS + place_col.astype(jnp.int32)
        meta_out[way] = jnp.minimum(dot(spread, one_hot(place_lane, far_place)), 1.0).astype(BF16)
        to_ring(way, way, meta_out, meta_in, meta_send, meta_recv)

    @pl.when(sec == sections - 1)
    def _():
        zeros[...] = jnp.zeros_like(zeros)
        for c in range(CHUNKS):
            rows = pl.ds(c * chunk, chunk)
            pltpu.make_async_copy(zeros, passed_ref.at[0, rows], zero_sem.at[c]).start()

    def slots(j):
        @pl.when(sec > 0)
        def _():
            drain(grad_part.at[j], quarter_recv.at[j])

        slots_out[j] = dot(by_slot[j % 2], grad_part[j]).astype(BF16)
        to_ring(j % 2, j, slots_out, slots_in, slots_send, slots_recv)

    def learn_places(way):
        ring_wait(way, meta_in, meta_recv)
        turned = meta_in[way].astype(F32).T[0:places].astype(BF16)
        meta_turned[way] = turned
        if way == 0:
            part_out[0, :, pl.ds(part, LANES)] = dot(turned, jnp.ones((all_slots, LANES), BF16))

    def part_cols(j):
        return pl.ds(0, part + LANES if j == 0 else part)

    def parts(j):
        way = j % 2
        ring_wait(j, slots_in, slots_recv)
        part_out[j, :, pl.ds(0, part)] = dot(meta_turned[way], slots_in[j])
        cols = part_cols(j)

        @pl.loop(0, ring - 1)
        def _(k):
            q = (line_me[way] + farthest_first(k, ring)) % ring
            theirs = pl.ds(pl.multiple_of(q * ROWS, ROWS), ROWS)
            send(
                part_out.at[j, theirs, cols],
                part_in.at[j, line_me[way], :, cols],
                part_send.at[j],
                part_recv.at[j],
                sec,
                line_peer[way](q),
            )

        mine = pl.ds(pl.multiple_of(line_me[way] * ROWS, ROWS), ROWS)
        part_in[j, line_me[way], :, cols] = part_out[j, mine, cols]

    def update(j, hits):
        way = j % 2
        drain(part_in.at[j, pl.ds(0, ring - 1), :, part_cols(j)], part_recv.at[j])
        total = part_in[j, 0, :, part_cols(j)]
        for q in range(1, ring):
            total += part_in[j, q, :, part_cols(j)]
        if j == 0:
            hits = total[:, part : part + 1]
        cols = pl.ds(j * part, part)
        table, first, second = adam_rows(
            hits > 0.5, total[:, 0:part], table_ref[:, cols], first_ref[:, cols], second_ref[:, cols]
        )
        rows_out[j] = jnp.concatenate([table[:, 0:mid], table[:, mid:part]], axis=0).astype(BF16)

        @pl.loop(0, ring - 1)
        def _(k):
            q = (line_me[way] + farthest_first(k, ring)) % ring
            send(
                rows_out.at[j],
                rows_in.at[j, line_me[way]],
                rows_send.at[j],
                rows_recv.at[j],
                sec,
                line_peer[way](q),
            )

        rows_in[j, line_me[way]] = rows_out[j]
        new_table_ref[:, cols] = table
        new_first_ref[:, cols] = first
        new_second_ref[:, cols] = second
        return hits

    def give_back(j):
        way = j % 2
        drain(rows_in.at[j, pl.ds(0, ring - 1)], rows_recv.at[j])
        blocks = []
        for q in range(ring):
            packed = rows_in[j, q].astype(F32)
            blocks.append(jnp.concatenate([packed[0:ROWS], packed[ROWS : 2 * ROWS]], axis=1))
        table = jnp.concatenate(blocks, axis=0).astype(BF16)
        back_out[j] = dot(meta_in[way, :, pl.ds(0, places)], table).astype(BF16)
        to_ring(way, j, back_out, back_in, back_send, back_recv)

    def fresh(j):
        ring_wait(j, back_in, back_recv)
        fresh_ref[:, pl.ds(j * part, part)] = dot(by_token[j % 2], back_in[j])

    def learn():
        for way in range(2):
            learn_places(way)
            by_token[way] = one_hot(slot_lane, slot_index(keeper_col, slot_col, way))
        for copy in small[3:]:
            copy.wait()

    for j in range(PARTS):
        slots(j)
    learn()
    for j in range(PARTS):
        parts(j)
    hits = None
    for j in range(PARTS):
        hits = update(j, hits)
    for j in range(PARTS):
        give_back(j)
    for j in range(PARTS):
        fresh(j)

    @pl.when(sec == 0)
    def _():
        drain(grad.at[:, pl.ds(0, width - quarter)], quarter_send)

    @pl.when(sec > 0)
    def _():
        drain(grad, passed_send)

    @pl.when(sec < sections - 1)
    def _():
        drain(passed_ref.at[0], passed_recv)

    @pl.when(sec == sections - 1)
    def _():
        for c in range(CHUNKS):
            rows = pl.ds(c * chunk, chunk)
            pltpu.make_async_copy(zeros, passed_ref.at[0, rows], zero_sem.at[c]).wait()

    for way in range(2):
        ring_wait(way, meta_out, meta_send)
    for j in range(PARTS):
        ring_wait(j, slots_out, slots_send)
        ring_wait(j, back_out, back_send)
        drain(part_in.at[j, pl.ds(0, ring - 1), :, part_cols(j)], part_send.at[j])
        drain(rows_in.at[j, pl.ds(0, ring - 1)], rows_send.at[j])


def hand_out(*refs):
    ins, outs, sems = refs[:5], refs[5:10], refs[10]
    copies = [pltpu.make_async_copy(a, b, sems.at[k]) for k, (a, b) in enumerate(zip(ins, outs))]
    for copy in copies:
        copy.start()
    for copy in copies:
        copy.wait()


def shards(
    ring,
    saved_input,
    upstream,
    cotangent,
    norm_gain,
    token_ids,
    piece_home,
    piece_table,
    first_moment,
    second_moment,
):
    _, tokens, width = saved_input.shape
    rows, quarter = piece_table.shape
    part = quarter // PARTS
    peers = 2 * ring
    slots = peers * peers
    hbm = pl.BlockSpec(memory_space=pltpu.HBM)
    anywhere = pl.BlockSpec(memory_space=pl.ANY)
    vmem = pl.BlockSpec(memory_space=pltpu.VMEM)
    dma = pltpu.SemaphoreType.DMA
    small = jax.ShapeDtypeStruct((rows, quarter), F32)
    out_shape = (
        jax.ShapeDtypeStruct((1, tokens, width), BF16),
        jax.ShapeDtypeStruct((tokens, quarter), F32),
        small,
        small,
        small,
    )
    arrays = (
        saved_input,
        upstream,
        cotangent,
        norm_gain,
        token_ids[None, :],
        piece_home[None, :],
        piece_table,
        first_moment,
        second_moment,
    )
    results = pl.pallas_call(
        functools.partial(kernel, ring),
        out_shape=out_shape,
        in_specs=[hbm] * 9,
        out_specs=(anywhere, vmem, vmem, vmem, vmem),
        scratch_shapes=[
            pltpu.VMEM((tokens, width), BF16),
            pltpu.VMEM((tokens, width), BF16),
            pltpu.VMEM((tokens, width), BF16),
            pltpu.VMEM((1, width), BF16),
            pltpu.VMEM((1, tokens), jnp.int32),
            pltpu.VMEM((1, piece_home.shape[0]), jnp.int32),
            pltpu.VMEM((rows, quarter), F32),
            pltpu.VMEM((rows, quarter), F32),
            pltpu.VMEM((rows, quarter), F32),
            pltpu.VMEM((tokens, width), BF16),
            pltpu.VMEM((tokens // CHUNKS, width), BF16),
            pltpu.VMEM((PARTS, tokens, part), BF16),
            pltpu.VMEM((2, slots, tokens), BF16),
            pltpu.VMEM((2, tokens, slots), BF16),
            pltpu.VMEM((2, slots, LANES), BF16),
            pltpu.VMEM((2, slots, LANES), BF16),
            pltpu.VMEM((2, ring * ROWS, slots), BF16),
            pltpu.VMEM((PARTS, slots, part), BF16),
            pltpu.VMEM((PARTS, slots, part), BF16),
            pltpu.VMEM((PARTS, ring * ROWS, part + LANES), F32),
            pltpu.VMEM((PARTS, ring, ROWS, part + LANES), F32),
            pltpu.VMEM((PARTS, 2 * ROWS, part // 2), BF16),
            pltpu.VMEM((PARTS, ring, 2 * ROWS, part // 2), BF16),
            pltpu.VMEM((PARTS, slots, part), BF16),
            pltpu.VMEM((PARTS, slots, part), BF16),
            dma((CHUNKS, 3)),
            dma((6,)),
            dma((CHUNKS,)),
            dma,
            dma((PARTS,)),
            dma,
            dma,
            dma((2,)),
            dma((2,)),
        ]
        + [dma((PARTS,))] * 8,
        compiler_params=pltpu.CompilerParams(
            collective_id=0, has_side_effects=True, vmem_limit_bytes=40 * 2**20
        ),
        cost_estimate=pl.CostEstimate(
            flops=2 * 10**8, bytes_accessed=6 * 2**20, transcendentals=0
        ),
    )(*(pltpu.with_memory_space_constraint(array, pltpu.HBM) for array in arrays))
    return pl.pallas_call(
        hand_out,
        out_shape=out_shape,
        in_specs=[anywhere] * 5,
        out_specs=(hbm,) * 5,
        scratch_shapes=[dma((5,))],
        compiler_params=pltpu.CompilerParams(vmem_limit_bytes=40 * 2**20),
        cost_estimate=pl.CostEstimate(flops=0, bytes_accessed=3 * 2**20, transcendentals=0),
    )(*results)


def solution(mesh):
    ring = math.isqrt(mesh.shape["dp"] // 2)
    in_specs = (
        P("section", "dp", None),
        P("section", "dp", None),
        P("section", "dp", None),
        P("section", None),
        P("dp"),
        P(),
        P("dp", "section"),
        P("dp", "section"),
        P("dp", "section"),
    )
    out_specs = (
        P("section", "dp", None),
        P("dp", "section"),
        P("dp", "section"),
        P("dp", "section"),
        P("dp", "section"),
    )
    return jax.shard_map(
        functools.partial(shards, ring),
        mesh=mesh,
        in_specs=in_specs,
        out_specs=out_specs,
        check_vma=False,
    )
```

time: 62.5 us -> 50.6 us (0.81)
  Pallas kernels: 61.7 us -> 49.8 us
    pallas_call x1, Pallas kernels: 60.5 us -> 48.6 us  [shards(): pl.pallas_call(functools.partial(kernel, ring), out_shape=out_shape, in_s...]
where the time goes in v3:
time: 50.6 us; the launch traced here: 50.4 us
  Pallas kernels  49.8 us (98%)
  between operations  0.64 us (1%)
    pallas_call x1, Pallas kernels, shards(): pl.pallas_call(functools.partial(kernel, ring), out_shape=out_shape, in_s...  48.6 us
    pallas_call x1, Pallas kernels, shards(): pl.pallas_call(hand_out, out_shape=out_shape, in_specs=[anywhere] * 5, ou...  1.2 us

profile of v3, /device:TPU:5, one launch (start us, length us, event | category | flops | bytes accessed | tf_op | source)
XLA Modules:
  0.0 50.4 jit_solution(15827250233343324573)
XLA Ops:
  0.6 48.6 %shard_map.128 = (bf16[1,128,4096]{2,1,0:T(8,128)(2,1)S(1)}, f32[128,1024]{1,0:T(8,128)S(1)}, f32[8,1024]{1,0:T(8,128)S(1)}, f32[8,1024]{1,0:T(8,128)S(1)}, f32[8,1024]{1,0:T(8,128)S(1)}) custom-call(bf16[1,128,4096]{2,1,0:T(8,128)(2,1)} %x_hbm.1, bf16[1,128,4096]{2,1,0:T(8,128)(2,1)} %up_hbm.1, bf16[1,128,4096]{2,1,0:T(8,128)(2,1)} %ct_hbm.1, ...), custom_call_target="tpu_custom_call" | custom-call | flops 200000000 | bytes 6291456 | tf_op jit(solution)/shard_map/pallas_call | solution.py:485
  49.2 1.2 %shard_map.129 = (bf16[1,128,4096]{2,1,0:T(8,128)(2,1)}, f32[128,1024]{1,0:T(8,128)}, f32[8,1024]{1,0:T(8,128)}, f32[8,1024]{1,0:T(8,128)}, f32[8,1024]{1,0:T(8,128)}) custom-call(bf16[1,128,4096]{2,1,0:T(8,128)(2,1)S(1)} %get-tuple-element.10.refs_0_, f32[128,1024]{1,0:T(8,128)S(1)} %get-tuple-element.11.refs_1_, f32[8,1024]{1,0:T(8,128)S(1)} %get-tuple-element.12.refs_2_, ...), custom_call_target="tpu_custom_call" | custom-call | bytes 3145728 | tf_op jit(solution)/shard_map/pallas_call | solution.py:534

commit v4 on v3

--- a/solution.py
+++ b/solution.py
@@ -25,6 +25,8 @@
 LANES = 128
 CHUNKS = 4
 PARTS = 4
+EXTRA = ((2, 2), (2, 3))
+BUFFERS = PARTS + len(EXTRA)
 
 
 def dot(a, b):
@@ -84,6 +86,9 @@
     slots_in,
     part_out,
     part_in,
+    row_sums,
+    total_out,
+    total_in,
     rows_out,
     rows_in,
     back_out,
@@ -105,6 +110,8 @@
     rows_recv,
     back_send,
     back_recv,
+    total_send,
+    total_recv,
 ):
     peers = 2 * ring
     all_slots = peers * peers
@@ -237,6 +244,24 @@
 
     last = sections - 1
 
+    def has_no(j):
+        owners = [d for d, k in EXTRA if k == j]
+        if not owners:
+            return None
+        return functools.reduce(jnp.logical_or, [sec == d for d in owners])
+
+    def where_summed(b, run):
+        left = None if b >= PARTS else has_no(b)
+        if b >= PARTS:
+            pl.when(sec == 0)(run)
+        elif left is None:
+            run()
+        else:
+            pl.when(jnp.logical_not(left))(run)
+
+    def part_of(b):
+        return b if b < PARTS else EXTRA[b - PARTS][1]
+
     def send_quarter(d, j):
         cols = pl.ds(d * quarter + j * part, part)
         send(grad.at[:, cols], grad_part.at[j], quarter_send, quarter_recv.at[j], d, dp)
@@ -245,9 +270,12 @@
     def _():
         for j in range(PARTS):
             for d in range(1, sections):
-                send_quarter(d, j)
+                if (d, j) not in EXTRA:
+                    send_quarter(d, j)
         for j in range(PARTS):
             grad_part[j] = grad[:, pl.ds(j * part, part)]
+        for e, (d, j) in enumerate(EXTRA):
+            grad_part[PARTS + e] = grad[:, pl.ds(d * quarter + j * part, part)]
 
     @pl.when(sec > 0)
     def _():
@@ -299,59 +327,108 @@
             rows = pl.ds(c * chunk, chunk)
             pltpu.make_async_copy(zeros, passed_ref.at[0, rows], zero_sem.at[c]).start()
 
-    def slots(j):
-        @pl.when(sec > 0)
-        def _():
-            drain(grad_part.at[j], quarter_recv.at[j])
-
-        slots_out[j] = dot(by_slot[j % 2], grad_part[j]).astype(BF16)
-        to_ring(j % 2, j, slots_out, slots_in, slots_send, slots_recv)
+    def slots(b):
+        way = part_of(b) % 2
+
+        def run():
+            if b < PARTS:
+
+                @pl.when(sec > 0)
+                def _():
+                    drain(grad_part.at[b], quarter_recv.at[b])
+
+            slots_out[b] = dot(by_slot[way], grad_part[b]).astype(BF16)
+            to_ring(way, b, slots_out, slots_in, slots_send, slots_recv)
+
+        where_summed(b, run)
 
     def learn_places(way):
         ring_wait(way, meta_in, meta_recv)
         turned = meta_in[way].astype(F32).T[0:places].astype(BF16)
         meta_turned[way] = turned
         if way == 0:
-            part_out[0, :, pl.ds(part, LANES)] = dot(turned, jnp.ones((all_slots, LANES), BF16))
-
-    def part_cols(j):
-        return pl.ds(0, part + LANES if j == 0 else part)
-
-    def parts(j):
-        way = j % 2
-        ring_wait(j, slots_in, slots_recv)
-        part_out[j, :, pl.ds(0, part)] = dot(meta_turned[way], slots_in[j])
-        cols = part_cols(j)
-
-        @pl.loop(0, ring - 1)
-        def _(k):
-            q = (line_me[way] + farthest_first(k, ring)) % ring
-            theirs = pl.ds(pl.multiple_of(q * ROWS, ROWS), ROWS)
-            send(
-                part_out.at[j, theirs, cols],
-                part_in.at[j, line_me[way], :, cols],
-                part_send.at[j],
-                part_recv.at[j],
-                sec,
-                line_peer[way](q),
-            )
-
-        mine = pl.ds(pl.multiple_of(line_me[way] * ROWS, ROWS), ROWS)
-        part_in[j, line_me[way], :, cols] = part_out[j, mine, cols]
+            hits = dot(turned, jnp.ones((all_slots, LANES), BF16))
+            none = jnp.zeros((ROWS, LANES), F32)
+            packed = [x for q in range(ring) for x in (hits[q * ROWS : (q + 1) * ROWS], none)]
+            part_out[0, :, pl.ds(mid, LANES)] = jnp.concatenate(packed, axis=0).astype(BF16)
+
+    def part_cols(b):
+        return pl.ds(0, mid + LANES if b == 0 else mid)
+
+    def pack(rows):
+        return jnp.concatenate([rows[:, 0:mid], rows[:, mid:part]], axis=0)
+
+    def unpack(rows):
+        return jnp.concatenate([rows[0:ROWS, 0:mid], rows[ROWS : 2 * ROWS, 0:mid]], axis=1)
+
+    def parts(b):
+        way = part_of(b) % 2
+        cols = part_cols(b)
+
+        def run():
+            ring_wait(b, slots_in, slots_recv)
+            sums = dot(meta_turned[way], slots_in[b])
+            packed = [pack(sums[q * ROWS : (q + 1) * ROWS]) for q in range(ring)]
+            part_out[b, :, pl.ds(0, mid)] = jnp.concatenate(packed, axis=0).astype(BF16)
+
+            @pl.loop(0, ring - 1)
+            def _(k):
+                q = (line_me[way] + farthest_first(k, ring)) % ring
+                theirs = pl.ds(pl.multiple_of(q * 2 * ROWS, 2 * ROWS), 2 * ROWS)
+                send(
+                    part_out.at[b, theirs, cols],
+                    part_in.at[b, line_me[way], :, cols],
+                    part_send.at[b],
+                    part_recv.at[b],
+                    sec,
+                    line_peer[way](q),
+                )
+
+            mine = pl.ds(pl.multiple_of(line_me[way] * 2 * ROWS, 2 * ROWS), 2 * ROWS)
+            part_in[b, line_me[way], :, cols] = part_out[b, mine, cols]
+
+        where_summed(b, run)
+
+    def total(b):
+        drain(part_in.at[b, pl.ds(0, ring - 1), :, part_cols(b)], part_recv.at[b])
+        rows = part_in[b, 0, :, part_cols(b)].astype(F32)
+        for q in range(1, ring):
+            rows += part_in[b, q, :, part_cols(b)].astype(F32)
+        return rows
+
+    def hand_total(e):
+        @pl.when(sec == 0)
+        def _():
+            total_out[e] = unpack(total(PARTS + e))
+            send(total_out.at[e], total_in.at[e], total_send.at[e], total_recv.at[e], EXTRA[e][0], dp)
 
     def update(j, hits):
         way = j % 2
-        drain(part_in.at[j, pl.ds(0, ring - 1), :, part_cols(j)], part_recv.at[j])
-        total = part_in[j, 0, :, part_cols(j)]
-        for q in range(1, ring):
-            total += part_in[j, q, :, part_cols(j)]
-        if j == 0:
-            hits = total[:, part : part + 1]
+        if has_no(j) is None:
+            rows = total(j)
+            sums = unpack(rows)
+            if j == 0:
+                hits = rows[0:ROWS, mid : mid + 1]
+        else:
+
+            def run():
+                row_sums[...] = unpack(total(j))
+
+            where_summed(j, run)
+            for e, (d, k) in enumerate(EXTRA):
+                if k == j:
+
+                    @pl.when(sec == d)
+                    def _():
+                        drain(total_in.at[e], total_recv.at[e])
+                        row_sums[...] = total_in[e]
+
+            sums = row_sums[...]
         cols = pl.ds(j * part, part)
         table, first, second = adam_rows(
-            hits > 0.5, total[:, 0:part], table_ref[:, cols], first_ref[:, cols], second_ref[:, cols]
+            hits > 0.5, sums, table_ref[:, cols], first_ref[:, cols], second_ref[:, cols]
         )
-        rows_out[j] = jnp.concatenate([table[:, 0:mid], table[:, mid:part]], axis=0).astype(BF16)
+        rows_out[j] = pack(table).astype(BF16)
 
         @pl.loop(0, ring - 1)
         def _(k):
@@ -374,10 +451,7 @@
     def give_back(j):
         way = j % 2
         drain(rows_in.at[j, pl.ds(0, ring - 1)], rows_recv.at[j])
-        blocks = []
-        for q in range(ring):
-            packed = rows_in[j, q].astype(F32)
-            blocks.append(jnp.concatenate([packed[0:ROWS], packed[ROWS : 2 * ROWS]], axis=1))
+        blocks = [unpack(rows_in[j, q].astype(F32)) for q in range(ring)]
         table = jnp.concatenate(blocks, axis=0).astype(BF16)
         back_out[j] = dot(meta_in[way, :, pl.ds(0, places)], table).astype(BF16)
         to_ring(way, j, back_out, back_in, back_send, back_recv)
@@ -393,12 +467,15 @@
         for copy in small[3:]:
             copy.wait()
 
-    for j in range(PARTS):
-        slots(j)
+    buffers = (*range(PARTS, PARTS + len(EXTRA)), *range(PARTS))
+    for b in buffers:
+        slots(b)
     learn()
-    for j in range(PARTS):
-        parts(j)
+    for b in buffers:
+        parts(b)
     hits = None
+    for e in range(len(EXTRA)):
+        hand_total(e)
     for j in range(PARTS):
         hits = update(j, hits)
     for j in range(PARTS):
@@ -408,7 +485,7 @@
 
     @pl.when(sec == 0)
     def _():
-        drain(grad.at[:, pl.ds(0, width - quarter)], quarter_send)
+        drain(grad.at[:, pl.ds(0, width - quarter - len(EXTRA) * part)], quarter_send)
 
     @pl.when(sec > 0)
     def _():
@@ -427,10 +504,20 @@
     for way in range(2):
         ring_wait(way, meta_out, meta_send)
     for j in range(PARTS):
-        ring_wait(j, slots_out, slots_send)
         ring_wait(j, back_out, back_send)
-        drain(part_in.at[j, pl.ds(0, ring - 1), :, part_cols(j)], part_send.at[j])
         drain(rows_in.at[j, pl.ds(0, ring - 1)], rows_send.at[j])
+    for b in buffers:
+
+        def sent():
+            ring_wait(b, slots_out, slots_send)
+            drain(part_in.at[b, pl.ds(0, ring - 1), :, part_cols(b)], part_send.at[b])
+
+        where_summed(b, sent)
+
+    @pl.when(sec == 0)
+    def _():
+        for e in range(len(EXTRA)):
+            drain(total_out.at[e], total_send.at[e])
 
 
 def hand_out(*refs):
@@ -499,16 +586,19 @@
             pltpu.VMEM((rows, quarter), F32),
             pltpu.VMEM((tokens, width), BF16),
             pltpu.VMEM((tokens // CHUNKS, width), BF16),
-            pltpu.VMEM((PARTS, tokens, part), BF16),
+            pltpu.VMEM((BUFFERS, tokens, part), BF16),
             pltpu.VMEM((2, slots, tokens), BF16),
             pltpu.VMEM((2, tokens, slots), BF16),
             pltpu.VMEM((2, slots, LANES), BF16),
             pltpu.VMEM((2, slots, LANES), BF16),
             pltpu.VMEM((2, ring * ROWS, slots), BF16),
-            pltpu.VMEM((PARTS, slots, part), BF16),
-            pltpu.VMEM((PARTS, slots, part), BF16),
-            pltpu.VMEM((PARTS, ring * ROWS, part + LANES), F32),
-            pltpu.VMEM((PARTS, ring, ROWS, part + LANES), F32),
+            pltpu.VMEM((BUFFERS, slots, part), BF16),
+            pltpu.VMEM((BUFFERS, slots, part), BF16),
+            pltpu.VMEM((BUFFERS, ring * 2 * ROWS, part // 2 + LANES), BF16),
+            pltpu.VMEM((BUFFERS, ring, 2 * ROWS, part // 2 + LANES), BF16),
+            pltpu.VMEM((ROWS, part), F32),
+            pltpu.VMEM((len(EXTRA), ROWS, part), F32),
+            pltpu.VMEM((len(EXTRA), ROWS, part), F32),
             pltpu.VMEM((PARTS, 2 * ROWS, part // 2), BF16),
             pltpu.VMEM((PARTS, ring, 2 * ROWS, part // 2), BF16),
             pltpu.VMEM((PARTS, slots, part), BF16),
@@ -523,7 +613,9 @@
             dma((2,)),
             dma((2,)),
         ]
-        + [dma((PARTS,))] * 8,
+        + [dma((BUFFERS,))] * 4
+        + [dma((PARTS,))] * 4
+        + [dma((len(EXTRA),))] * 2,
         compiler_params=pltpu.CompilerParams(
             collective_id=0, has_side_effects=True, vmem_limit_bytes=40 * 2**20
         ),

time: 50.6 us -> 47.1 us (0.931)
  the two profiles are of different devices: /device:TPU:5 before, /device:TPU:3 now
where the time goes in v4:
time: 47.1 us; the launch traced here: 46.9 us
  Pallas kernels  46.3 us (98%)
  between operations  0.64 us (1%)
    pallas_call x1, Pallas kernels, shards(): pl.pallas_call(functools.partial(kernel, ring), out_shape=out_shape, in_s...  45.1 us
    pallas_call x1, Pallas kernels, shards(): pl.pallas_call(hand_out, out_shape=out_shape, in_specs=[anywhere] * 5, ou...  1.2 us

profile of v4, /device:TPU:3, one launch (start us, length us, event | category | flops | bytes accessed | tf_op | source)
XLA Modules:
  0.0 46.9 jit_solution(8989562573519373175)
XLA Ops:
  0.6 45.1 %shard_map.128 = (bf16[1,128,4096]{2,1,0:T(8,128)(2,1)S(1)}, f32[128,1024]{1,0:T(8,128)S(1)}, f32[8,1024]{1,0:T(8,128)S(1)}, f32[8,1024]{1,0:T(8,128)S(1)}, f32[8,1024]{1,0:T(8,128)S(1)}) custom-call(bf16[1,128,4096]{2,1,0:T(8,128)(2,1)} %x_hbm.1, bf16[1,128,4096]{2,1,0:T(8,128)(2,1)} %up_hbm.1, bf16[1,128,4096]{2,1,0:T(8,128)(2,1)} %ct_hbm.1, ...), custom_call_target="tpu_custom_call" | custom-call | flops 200000000 | bytes 6291456 | tf_op jit(solution)/shard_map/pallas_call | solution.py:572
  45.7 1.2 %shard_map.129 = (bf16[1,128,4096]{2,1,0:T(8,128)(2,1)}, f32[128,1024]{1,0:T(8,128)}, f32[8,1024]{1,0:T(8,128)}, f32[8,1024]{1,0:T(8,128)}, f32[8,1024]{1,0:T(8,128)}) custom-call(bf16[1,128,4096]{2,1,0:T(8,128)(2,1)S(1)} %get-tuple-element.10.refs_0_, f32[128,1024]{1,0:T(8,128)S(1)} %get-tuple-element.11.refs_1_, f32[8,1024]{1,0:T(8,128)S(1)} %get-tuple-element.12.refs_2_, ...), custom_call_target="tpu_custom_call" | custom-call | bytes 3145728 | tf_op jit(solution)/shard_map/pallas_call | solution.py:626

commit v5 on v4

--- a/solution.py
+++ b/solution.py
@@ -154,7 +154,7 @@
     def to_ring(way, j, out, into, send_sem, recv_sem):
         mine = pl.ds(pl.multiple_of(ring_me[way] * peers, peers), peers)
 
-        @pl.loop(0, peers - 1)
+        @pl.loop(0, peers - 1, unroll=True)
         def _(k):
             p = (ring_me[way] + farthest_first(k, peers)) % peers
             theirs = pl.ds(pl.multiple_of(p * peers, peers), peers)
@@ -371,7 +371,7 @@
             packed = [pack(sums[q * ROWS : (q + 1) * ROWS]) for q in range(ring)]
             part_out[b, :, pl.ds(0, mid)] = jnp.concatenate(packed, axis=0).astype(BF16)
 
-            @pl.loop(0, ring - 1)
+            @pl.loop(0, ring - 1, unroll=True)
             def _(k):
                 q = (line_me[way] + farthest_first(k, ring)) % ring
                 theirs = pl.ds(pl.multiple_of(q * 2 * ROWS, 2 * ROWS), 2 * ROWS)
@@ -430,7 +430,7 @@
         )
         rows_out[j] = pack(table).astype(BF16)
 
-        @pl.loop(0, ring - 1)
+        @pl.loop(0, ring - 1, unroll=True)
         def _(k):
             q = (line_me[way] + farthest_first(k, ring)) % ring
             send(
@@ -480,9 +480,6 @@
         hits = update(j, hits)
     for j in range(PARTS):
         give_back(j)
-    for j in range(PARTS):
-        fresh(j)
-
     @pl.when(sec == 0)
     def _():
         drain(grad.at[:, pl.ds(0, width - quarter - len(EXTRA) * part)], quarter_send)
@@ -504,7 +501,6 @@
     for way in range(2):
         ring_wait(way, meta_out, meta_send)
     for j in range(PARTS):
-        ring_wait(j, back_out, back_send)
         drain(rows_in.at[j, pl.ds(0, ring - 1)], rows_send.at[j])
     for b in buffers:
 
@@ -518,6 +514,11 @@
     def _():
         for e in range(len(EXTRA)):
             drain(total_out.at[e], total_send.at[e])
+
+    for j in range(PARTS):
+        fresh(j)
+    for j in range(PARTS):
+        ring_wait(j, back_out, back_send)
 
 
 def hand_out(*refs):

time: 47.1 us -> 46.7 us (level)
  the two profiles are of different devices: /device:TPU:3 before, /device:TPU:1 now
where the time goes in v5:
time: 46.7 us; the launch traced here: 46.6 us
  Pallas kernels  45.9 us (98%)
  between operations  0.64 us (1%)
    pallas_call x1, Pallas kernels, shards(): pl.pallas_call(functools.partial(kernel, ring), out_shape=out_shape, in_s...  44.7 us
    pallas_call x1, Pallas kernels, shards(): pl.pallas_call(hand_out, out_shape=out_shape, in_specs=[anywhere] * 5, ou...  1.2 us

profile of v5, /device:TPU:1, one launch (start us, length us, event | category | flops | bytes accessed | tf_op | source)
XLA Modules:
  0.0 46.6 jit_solution(16417592984672092067)
XLA Ops:
  0.6 44.7 %shard_map.128 = (bf16[1,128,4096]{2,1,0:T(8,128)(2,1)S(1)}, f32[128,1024]{1,0:T(8,128)S(1)}, f32[8,1024]{1,0:T(8,128)S(1)}, f32[8,1024]{1,0:T(8,128)S(1)}, f32[8,1024]{1,0:T(8,128)S(1)}) custom-call(bf16[1,128,4096]{2,1,0:T(8,128)(2,1)} %x_hbm.1, bf16[1,128,4096]{2,1,0:T(8,128)(2,1)} %up_hbm.1, bf16[1,128,4096]{2,1,0:T(8,128)(2,1)} %ct_hbm.1, ...), custom_call_target="tpu_custom_call" | custom-call | flops 200000000 | bytes 6291456 | tf_op jit(solution)/shard_map/pallas_call | solution.py:573
  45.4 1.2 %shard_map.129 = (bf16[1,128,4096]{2,1,0:T(8,128)(2,1)}, f32[128,1024]{1,0:T(8,128)}, f32[8,1024]{1,0:T(8,128)}, f32[8,1024]{1,0:T(8,128)}, f32[8,1024]{1,0:T(8,128)}) custom-call(bf16[1,128,4096]{2,1,0:T(8,128)(2,1)S(1)} %get-tuple-element.10.refs_0_, f32[128,1024]{1,0:T(8,128)S(1)} %get-tuple-element.11.refs_1_, f32[8,1024]{1,0:T(8,128)S(1)} %get-tuple-element.12.refs_2_, ...), custom_call_target="tpu_custom_call" | custom-call | bytes 3145728 | tf_op jit(solution)/shard_map/pallas_call | solution.py:627
